TPU v7x, 32 devices: a whole 2x2x4 slice. The times are simulated.
32 devices in a mesh: dp: 16 (over z, y, core), mp: 2 (over x).
Axes of the slice: x: 2, y: 2, z: 4, core: 2. Of those that a mesh axis runs over, the one named last changes fastest.
Arguments:
- queries: bfloat16 [8192, 1024], P('dp', 'mp'), may hold values from -20 to 20
- passages: bfloat16 [65536, 1024], P('dp', 'mp'), may hold values from -6 to 6
- positives: int32 [8192], P('dp'), may hold values from 0 to 4095, as said below
- negatives: int32 [16, 16], replicated, may hold values from -1 to 31, as said below
Outputs:
- losses: float32 [8192], P('dp')
- query_grad: float32 [8192, 1024], P('dp', 'mp')
- passage_grad: float32 [65536, 1024], P('dp', 'mp')
Inputs may be any that keep to these rules, and one draw needn't show every extreme that they name: Within each dp index the 512 positives of its query block are distinct. `negatives`: each row names between 4 and 16 blocks (entries >= 0); some row names 16.
All inputs are finite; a program needn't handle non-finite values.
Results may differ from a plain program's by a relative error of at most 0.0075.
Values may be sent and summed in bfloat16 or wider, within the bound.
A program may use at most 128 MiB of HBM per device.

v0:
```python
import jax
import jax.numpy as jnp
from jax import lax
from jax.sharding import PartitionSpec as P

PBS = 128


def combined_all(part, axis, combine):
    gathered = jax.tree.map(lambda a: lax.all_gather(a, axis), part)

    def take(source):
        return jax.tree.map(lambda a: lax.dynamic_index_in_dim(a, source, 0, False), gathered)

    return lax.fori_loop(
        1, lax.axis_size(axis), lambda source, state: combine(state, take(source)), take(0)
    )


def combine_stats(first, second):
    top = jnp.maximum(first[0], second[0])
    total = first[1] * jnp.exp(first[0] - top) + second[1] * jnp.exp(second[0] - top)
    return (top, total, first[2] + second[2])


def body(queries, passages, positives, negatives):
    dp_count = lax.axis_size("dp")
    mp_count = lax.axis_size("mp")
    own_index = lax.axis_index("dp")
    shard_width = queries.shape[1]
    factor = (shard_width * mp_count) ** (-0.5)
    query_rows = queries.shape[0]
    block_count = passages.shape[0] // PBS
    blocks = passages.reshape(block_count, PBS, shard_width)
    asked = lax.dynamic_index_in_dim(negatives, own_index, 1, keepdims=False)
    outgoing = jnp.take(blocks, jnp.maximum(asked, 0), axis=0)
    outgoing = jnp.where((asked >= 0)[:, None, None], outgoing, jnp.zeros_like(outgoing))
    fetched = lax.all_to_all(outgoing, "dp", split_axis=0, concat_axis=0, tiled=True)
    wanted = lax.dynamic_index_in_dim(negatives, own_index, 0, keepdims=False)
    positive_rows = jnp.take(passages, positives, axis=0)
    cands = jnp.concatenate([positive_rows, fetched.reshape(dp_count * PBS, shard_width)], 0)
    share = cands.shape[0] // mp_count
    width_index = lax.axis_index("mp")
    row_ids = width_index * share + jnp.arange(share, dtype=jnp.int32)
    slot_ids = (row_ids - query_rows) // PBS
    present = jnp.any(
        (slot_ids[:, None] == jnp.arange(dp_count, dtype=jnp.int32)[None, :])
        & (wanted >= 0)[None, :],
        axis=1,
    )
    valid = (row_ids < query_rows) | present
    target = row_ids[:, None] == jnp.arange(query_rows, dtype=jnp.int32)[None, :]
    scores = factor * lax.psum_scatter(
        lax.dot_general(
            cands, queries, (((1,), (1,)), ((), ())), preferred_element_type=jnp.float32
        ),
        "mp",
        scatter_dimension=0,
        tiled=True,
    )
    masked = jnp.where(valid[:, None], scores, jnp.float32(-1e30))
    local_top = jnp.max(masked, axis=0)
    local_total = jnp.sum(
        jnp.where(valid[:, None], jnp.exp(masked - local_top), jnp.float32(0.0)), axis=0
    )
    local_own = jnp.sum(jnp.where(target, scores, jnp.float32(0.0)), axis=0)
    top, total, own_score = combined_all((local_top, local_total, local_own), "mp", combine_stats)
    lse = top + jnp.log(total)
    losses = lse - own_score
    prob = jnp.where(valid[:, None], jnp.exp(masked - lse), jnp.float32(0.0))
    grad_scores = (prob - target.astype(jnp.float32)).astype(jnp.bfloat16)
    all_grads = lax.all_gather(grad_scores, "mp", axis=0, tiled=True)
    query_grad = factor * lax.dot_general(
        all_grads, cands, (((0,), (0,)), ((), ())), preferred_element_type=jnp.float32
    )
    cand_grad = factor * jnp.dot(all_grads, queries, preferred_element_type=jnp.float32)
    sending = cand_grad[query_rows:].reshape(dp_count, PBS, shard_width)
    returned = lax.all_to_all(
        sending.astype(jnp.bfloat16), "dp", split_axis=0, concat_axis=0, tiled=True
    ).astype(sending.dtype)
    selector = (asked[None, :] == jnp.arange(block_count, dtype=jnp.int32)[:, None]).astype(
        jnp.float32
    )
    block_grad = jnp.einsum("kr,rpd->kpd", selector, returned, precision=lax.Precision.HIGHEST)
    passage_grad = (
        block_grad.reshape(block_count * PBS, shard_width).at[positives].add(cand_grad[:query_rows])
    )
    return (losses, query_grad, passage_grad)


def solution(mesh):
    in_specs = (P("dp", "mp"), P("dp", "mp"), P("dp"), P())
    out_specs = (P("dp"), P("dp", "mp"), P("dp", "mp"))
    return jax.shard_map(body, mesh=mesh, in_specs=in_specs, out_specs=out_specs, check_vma=False)
```

profile of v0, /device:TPU:13, one launch (start us, length us, event | category | flops | bytes accessed | tf_op | source)
XLA Modules:
  0.0 280.8 jit_solution(18013359425366005172)
XLA Ops:
  7.2 0.0 copy-start
  7.2 0.9 compare_reduce_fusion
  8.1 0.9 dynamic-slice_reduce_fusion
  9.0 2.9 %gather_fusion.1 = bf16[16,128,512]{2,1,0:T(8,128)(2,1)S(1)} fusion(bf16[32,128,512]{2,1,0:T(8,128)(2,1)} %bitcast.51, s32[1024]{0:T(1024)S(1)} %pad_clamp_fusion), kind=kCustom, calls=%fused_computation.1 | custom fusion | bytes 4194368 | tf_op jit(solution)/shard_map/jit(_take)/gather | solution.py:36
  11.9 1.6 select_select_fusion
  13.5 0.0 copy-start.5
  13.5 6.7 %all-to-all-start = ((bf16[16,128,512]{2,1,0:T(8,128)(2,1)}), bf16[16,128,512]{2,1,0:T(8,128)(2,1)S(1)}, u32[]{:S(2)}, u32[]{:S(2)}) async-start(bf16[16,128,512]{2,1,0:T(8,128)(2,1)} %select_select_fusion), calls=%async_computation | async-start | bytes 4194304 | tf_op jit(solution)/shard_map/all_to_all | solution.py:38
  20.2 0.0 reduce-scatter.2.cloned.1.call-start
  20.3 0.0 copy-done.5
  20.3 4.7 %gather_fusion = bf16[512,512]{1,0:T(8,128)(2,1)S(1)} fusion(bf16[4096,512]{1,0:T(8,128)(2,1)} %param.5, s32[1024]{0:T(1024)S(1)} %pad_clamp_fusion.1), kind=kCustom, calls=%fused_computation | custom fusion | bytes 1050624 | tf_op jit(solution)/shard_map/jit(_take)/gather | solution.py:40
  25.0 0.9 broadcast_select_fusion
  26.0 41.7 %all-to-all-done = bf16[16,128,512]{2,1,0:T(8,128)(2,1)S(1)} async-done(((bf16[16,128,512]{2,1,0:T(8,128)(2,1)}), bf16[16,128,512]{2,1,0:T(8,128)(2,1)S(1)}, u32[]{:S(2)}, u32[]{:S(2)}) %all-to-all-start) | async-done | bytes 2097184 | tf_op jit(solution)/shard_map/all_to_all | solution.py:38
  67.6 0.0 copy-start.3
  67.6 0.0 copy-done
  67.6 5.3 %fusion.4 = f32[2560,512]{1,0:T(8,128)} fusion(bf16[512,512]{1,0:T(8,128)(2,1)S(1)} %copy-done, bf16[2048,512]{1,0:T(8,128)(2,1)S(1)} %bitcast.53, bf16[512,512]{1,0:T(8,128)(2,1)} %broadcast_select_fusion), kind=kOutput, calls=%fused_computation.16 | convolution fusion | flops 1347420160 | bytes 8388608 | tf_op jit(solution)/shard_map/dot_general | solution.py:54
  73.0 0.0 copy-done.3
  73.0 0.0 reduce-scatter.2.cloned.1.call-update
  73.0 0.0 all-gather.8.cloned.1.call-start
  73.0 0.7 compare_bitcast_fusion
  73.8 0.1 fusion.9
  73.9 64.4 %reduce-scatter.2.cloned.1.call-done = f32[1280,512]{1,0:T(8,128)} async-done(((f32[2560,512]{1,0:T(8,128)}), f32[1280,512]{1,0:T(8,128)}) %reduce-scatter.2.cloned.1.call-update) | async-done | bytes 2621456 | tf_op jit(solution)/shard_map/reduce_scatter | solution.py:53
  138.3 0.0 copy-start.1
  138.3 2.3 fusion.2
  140.5 3.2 %all-gather.3 = f32[2,1,512]{2,1,0:T(1,128)S(1)} all-gather(f32[1,1,512]{2,1,0:T(1,128)S(1)} %bitcast.55), channel_id=2, replica_groups=mesh['dp'=16,'mp'=2] {'mp'}, dimensions={0}, use_global_device_ids=true | all-gather | bytes 6144 | tf_op jit(solution)/shard_map/all_gather | solution.py:10
  143.7 0.0 copy-done.1
  143.7 1.4 select_reduce_fusion.1
  145.1 3.2 %all-gather.4 = f32[2,1,512]{2,1,0:T(1,128)S(1)} all-gather(f32[1,1,512]{2,1,0:T(1,128)S(1)} %bitcast.57), channel_id=3, replica_groups=mesh['dp'=16,'mp'=2] {'mp'}, dimensions={0}, use_global_device_ids=true | all-gather | bytes 6144 | tf_op jit(solution)/shard_map/all_gather | solution.py:10
  148.3 2.1 subtract_convert_fusion
  150.4 0.0 all-gather.8.cloned.1.call-update
  150.5 41.5 %all-gather.8.cloned.1.call-done = bf16[2560,512]{1,0:T(8,128)(2,1)} async-done(((bf16[1280,512]{1,0:T(8,128)(2,1)}), bf16[2560,512]{1,0:T(8,128)(2,1)}) %all-gather.8.cloned.1.call-update) | async-done | bytes 2621456 | tf_op jit(solution)/shard_map/all_gather | solution.py:72
  191.9 3.3 %convolution_multiply_fusion = f32[2560,512]{1,0:T(8,128)S(1)} fusion(bf16[2560,512]{1,0:T(8,128)(2,1)} %all-gather.8.cloned.1.call-done, bf16[512,512]{1,0:T(8,128)(2,1)S(1)} %copy-done), kind=kOutput, calls=%fused_computation.3 | convolution fusion | flops 1343488000 | bytes 8388608 | tf_op jit(solution)/shard_map/dot_general | solution.py:76
  195.2 0.0 copy-start.2
  195.2 2.3 copy-done.2
  197.5 1.6 slice.48
  199.1 0.0 copy-start.4
  199.1 6.5 %all-to-all-start.1 = ((bf16[16,128,512]{2,1,0:T(8,128)(2,1)}), bf16[16,128,512]{2,1,0:T(8,128)(2,1)S(1)}, u32[]{:S(2)}, u32[]{:S(2)}) async-start(bf16[16,128,512]{2,1,0:T(8,128)(2,1)} %bitcast.17), calls=%async_computation.2 | async-start | bytes 4194304 | tf_op jit(solution)/shard_map/all_to_all | solution.py:78
  205.6 3.6 %all-gather.5 = f32[2,1,512]{2,1,0:T(1,128)S(1)} all-gather(f32[1,1,512]{2,1,0:T(1,128)S(1)} %bitcast.56), channel_id=4, replica_groups=mesh['dp'=16,'mp'=2] {'mp'}, dimensions={0}, use_global_device_ids=true | all-gather | bytes 6144 | tf_op jit(solution)/shard_map/all_gather | solution.py:10
  209.2 0.6 add_subtract_fusion
  209.8 0.0 copy-done.4
  209.8 4.9 %fusion.5 = f32[512,512]{1,0:T(8,128)} fusion(bf16[2560,512]{1,0:T(8,128)(2,1)} %all-gather.8.cloned.1.call-done, bf16[2048,512]{1,0:T(8,128)(2,1)} %bitcast.54, bf16[512,512]{1,0:T(8,128)(2,1)S(1)} %copy-done.4), kind=kOutput, calls=%fused_computation.17 | convolution fusion | flops 1347682304 | bytes 6291456 | tf_op jit(solution)/shard_map/dot_general | solution.py:73
  214.7 38.3 %all-to-all-done.1 = bf16[16,128,512]{2,1,0:T(8,128)(2,1)S(1)} async-done(((bf16[16,128,512]{2,1,0:T(8,128)(2,1)}), bf16[16,128,512]{2,1,0:T(8,128)(2,1)S(1)}, u32[]{:S(2)}, u32[]{:S(2)}) %all-to-all-start.1) | async-done | bytes 2097184 | tf_op jit(solution)/shard_map/all_to_all | solution.py:78
  253.0 1.6 fusion
  254.6 8.3 %copy.13 = f32[32,128,512]{2,1,0:T(8,128)} copy(f32[32,128,512]{2,0,1:T(8,128)S(1)} %fusion) | data formatting | bytes 16777216 | tf_op jit(solution)/shard_map/kr,rpd->kpd/dot_general | solution.py:84
  262.9 11.0 %scatter_custom_fusion = f32[4096,512]{1,0:T(8,128)} fusion(f32[4096,512]{1,0:T(8,128)} %bitcast.52, s32[512]{0:T(512)S(1)} %compare_select_fusion, f32[2560,512]{1,0:T(8,128)} %copy-done.2), kind=kCustom, calls=%fused_computation.18 | custom fusion | flops 262144 | bytes 9437184 | tf_op jit(solution)/shard_map/scatter-add | solution.py:86
  (12 shorter events, 0.1 us)
Async XLA Ops:
  7.2 60.5 %copy-start = (bf16[512,512]{1,0:T(8,128)(2,1)S(1)}, bf16[512,512]{1,0:T(8,128)(2,1)}, u32[]{:S(2)}) copy-start(bf16[512,512]{1,0:T(8,128)(2,1)} %param.4) | copy-start | bytes 1572868
  13.5 6.7 %copy-start.5 = (s32[512]{0:T(512)S(1)}, s32[512]{0:T(512)}, u32[]{:S(2)}) copy-start(s32[512]{0:T(512)} %param.6) | copy-start | bytes 6148
  13.5 54.1 %all-to-all-start = ((bf16[16,128,512]{2,1,0:T(8,128)(2,1)}), bf16[16,128,512]{2,1,0:T(8,128)(2,1)S(1)}, u32[]{:S(2)}, u32[]{:S(2)}) async-start(bf16[16,128,512]{2,1,0:T(8,128)(2,1)} %select_select_fusion), calls=%async_computation | async-start | bytes 4194304 | tf_op jit(solution)/shard_map/all_to_all | solution.py:38
  20.2 118.1 %reduce-scatter.2.cloned.1.call-start = ((), (), s32[]{:S(2)}) async-start(), calls=%async_computation.3 | async-start | bytes 7864320 | tf_op jit(solution)/shard_map/reduce_scatter | solution.py:53
  67.6 5.3 %copy-start.3 = (bf16[16,128,512]{2,1,0:T(8,128)(2,1)}, bf16[16,128,512]{2,1,0:T(8,128)(2,1)S(1)}, u32[]{:S(2)}) copy-start(bf16[16,128,512]{2,1,0:T(8,128)(2,1)S(1)} %all-to-all-done) | copy-start | bytes 6291460
  73.0 119.0 %all-gather.8.cloned.1.call-start = ((), (), s32[]{:S(2)}) async-start(), calls=%async_computation.4 | async-start | bytes 3932160 | tf_op jit(solution)/shard_map/all_gather | solution.py:72
  138.3 5.5 %copy-start.1 = (f32[1280,512]{1,0:T(8,128)S(1)}, f32[1280,512]{1,0:T(8,128)}, u32[]{:S(2)}) copy-start(f32[1280,512]{1,0:T(8,128)} %reduce-scatter.2.cloned.1.call-done) | copy-start | bytes 7864324
  195.2 2.3 copy-start.2
  199.1 10.7 %copy-start.4 = (bf16[512,512]{1,0:T(8,128)(2,1)S(1)}, bf16[512,512]{1,0:T(8,128)(2,1)}, u32[]{:S(2)}) copy-start(bf16[512,512]{1,0:T(8,128)(2,1)} %broadcast_select_fusion) | copy-start | bytes 1572868
  199.1 53.9 %all-to-all-start.1 = ((bf16[16,128,512]{2,1,0:T(8,128)(2,1)}), bf16[16,128,512]{2,1,0:T(8,128)(2,1)S(1)}, u32[]{:S(2)}, u32[]{:S(2)}) async-start(bf16[16,128,512]{2,1,0:T(8,128)(2,1)} %bitcast.17), calls=%async_computation.2 | async-start | bytes 4194304 | tf_op jit(solution)/shard_map/all_to_all | solution.py:78
Sparse Core Ops, SparseCore 0:
  73.1 65.1 reduce-scatter.1
  150.6 41.3 all-gather.7
where the time goes:
time: 281 us
  waiting for transfers between devices  186 us (66%)
  other arithmetic  22.6 us (8%)
  local copies, waits for them, and re-layouts  19.8 us (7%)
  matrix products  15.1 us (5%)
  between operations  14.2 us (5%)
  starting transfers between devices  13.3 us (5%)
  blocking collectives  9.95 us (4%)
    reduce_scatter x1, waiting for transfers between devices, body(): lax.psum_scatter(lax.dot_general(cands, queries, (((1,), (1,)), ((), ()))...  64.4 us
    all_to_all x1, waiting for transfers between devices, body(): lax.all_to_all(outgoing, 'dp', split_axis=0, concat_axis=0, tiled=True)  41.7 us
    all_gather x1, waiting for transfers between devices, body(): all_grads = lax.all_gather(grad_scores, 'mp', axis=0, tiled=True)  41.5 us
    all_to_all x1, waiting for transfers between devices, body(): lax.all_to_all(sending.astype(jnp.bfloat16), 'dp', split_axis=0, concat_a...  38.3 us
    scatter-add x1, other arithmetic, body(): block_grad.reshape(block_count * PBS, shard_width).at[positives]  11 us
    all_gather x3, blocking collectives, combined_all(): gathered = jax.tree.map(lambda a: lax.all_gather(a, axis), part)  9.95 us
    dot_general x1, local copies, waits for them, and re-layouts, body(): jnp.einsum('kr,rpd->kpd', selector, returned, precision=lax.Precision.HIG...  8.25 us
    all_to_all x1, starting transfers between devices, body(): lax.all_to_all(outgoing, 'dp', split_axis=0, concat_axis=0, tiled=True)  6.69 us
  transfers between devices with their start and end apart: 4, of which 4 were waited for; matrix products, arithmetic and copies ran while one was open for 4% of the time, Pallas kernels for 0%

commit v1 on v0

v1 whole, which is shorter than its diff:
```python
import functools

import jax
import jax.numpy as jnp
from jax import lax
from jax.experimental import pallas as pl
from jax.experimental.pallas import tpu as pltpu
from jax.sharding import PartitionSpec as P

PBS = 128
MESH = pl.DeviceIdType.MESH
F32 = jnp.float32
BF16 = jnp.bfloat16


def exchange_kernel(
    dp, mp, factor,
    neg, pos, q, passages,
    losses, query_grad, pos_grad, returned,
    table, sending, cands, others, q_other, scores, grads, back, stats, top_ref,
    load_sem, f_send, f_recv, x_send, x_recv, q_send, q_recv,
    s_send, s_recv, g_send, g_recv, r_send, r_recv,
):
    me = lax.axis_index("dp")
    mine = lax.axis_index("mp")
    rows, width = q.shape
    pos_blocks = rows // PBS
    neg_groups = dp // mp
    groups = (dp + pos_blocks) // mp
    half = neg_groups // 2

    def partner(s):
        out = me
        bit = 1
        while bit < dp:
            out = out + bit * ((s // bit) % 2) * (1 - 2 * ((me // bit) % 2))
            bit *= 2
        return out

    def peer(p):
        return lax.rem(mine + p, mp)

    def ordered(k):
        return (1 - k % 2) * half + k // 2

    def fetch(s):
        return pltpu.make_async_remote_copy(
            src_ref=sending.at[s], dst_ref=cands.at[s],
            send_sem=f_send.at[s], recv_sem=f_recv.at[s],
            device_id=(partner(s), mine), device_id_type=MESH)

    def give_back(s):
        return pltpu.make_async_remote_copy(
            src_ref=back.at[s], dst_ref=returned.at[s],
            send_sem=r_send.at[s], recv_sem=r_recv.at[s],
            device_id=(partner(s), mine), device_id_type=MESH)

    def relay(p, t):
        return pltpu.make_async_remote_copy(
            src_ref=cands.at[t * mp + peer(p)], dst_ref=others.at[p - 1, t],
            send_sem=x_send.at[p - 1, t], recv_sem=x_recv.at[p - 1, t],
            device_id=(me, peer(p)), device_id_type=MESH)

    def share_queries(p):
        return pltpu.make_async_remote_copy(
            src_ref=q, dst_ref=q_other.at[p - 1],
            send_sem=q_send.at[p - 1], recv_sem=q_recv.at[p - 1],
            device_id=(me, peer(p)), device_id_type=MESH)

    def share_stats(p):
        return pltpu.make_async_remote_copy(
            src_ref=stats.at[mine], dst_ref=stats.at[mine],
            send_sem=s_send.at[p - 1], recv_sem=s_recv.at[p - 1],
            device_id=(me, peer(p)), device_id_type=MESH)

    def share_grads(p, t):
        return pltpu.make_async_remote_copy(
            src_ref=grads.at[t * mp + mine], dst_ref=grads.at[t * mp + mine],
            send_sem=g_send.at[p - 1, t], recv_sem=g_recv.at[p - 1, t],
            device_id=(me, peer(p)), device_id_type=MESH)

    def stats_from(p):
        source = lax.rem(mine + mp - p, mp)
        return pltpu.make_async_remote_copy(
            src_ref=stats.at[source], dst_ref=stats.at[source],
            send_sem=s_send.at[p - 1], recv_sem=s_recv.at[p - 1],
            device_id=(me, peer(p)), device_id_type=MESH)

    def grads_from(p, t):
        source = lax.rem(mine + mp - p, mp)
        return pltpu.make_async_remote_copy(
            src_ref=grads.at[t * mp + source], dst_ref=grads.at[t * mp + source],
            send_sem=g_send.at[p - 1, t], recv_sem=g_recv.at[p - 1, t],
            device_id=(me, peer(p)), device_id_type=MESH)

    load = pltpu.make_async_copy(passages, table, load_sem)
    load.start()
    barrier = pltpu.get_barrier_semaphore()

    @pl.loop(1, dp)
    def _(s):
        pl.semaphore_signal(barrier, inc=1, device_id=(partner(s), mine), device_id_type=MESH)

    for p in range(1, mp):
        pl.semaphore_signal(barrier, inc=1, device_id=(me, peer(p)), device_id_type=MESH)
    load.wait()
    pl.semaphore_wait(barrier, dp - 1 + mp - 1)

    def block_for(s):
        return table[jnp.maximum(neg[partner(s), me], 0)]

    cands[0] = block_for(0)

    @pl.loop(0, neg_groups)
    def _(k):
        t = ordered(k)
        for c in range(mp):
            s = t * mp + c

            @pl.when(s > 0)
            def _():
                sending[s] = block_for(s)
                fetch(s).start()

    for p in range(1, mp):
        share_queries(p).start()

    query_grad[...] = jnp.zeros_like(query_grad)
    chunk = 4 * PBS

    @pl.loop(0, table.shape[0] // 4)
    def _(c):
        ids = lax.broadcasted_iota(jnp.int32, (rows, chunk), 1) + c * chunk
        pick = jnp.where(ids == pos[...], 1.0, 0.0).astype(BF16)
        part = table[pl.ds(c * 4, 4)].reshape(chunk, width)
        query_grad[...] += jnp.dot(pick, part, preferred_element_type=F32)

    for b in range(pos_blocks):
        cands[dp + b] = query_grad[b * PBS:(b + 1) * PBS, :].astype(BF16)
    for t in range(neg_groups, groups):
        for p in range(1, mp):
            relay(p, t).start()
    for p in range(1, mp):
        share_queries(p).wait_recv()

    top_ref[...] = jnp.full(top_ref.shape, -1e30, F32)

    def dot_nt(a, b):
        return lax.dot_general(a, b, (((1,), (1,)), ((), ())), preferred_element_type=F32)

    def score(t):
        total = dot_nt(cands[t * mp + mine], q[...])
        for p in range(1, mp):
            relay(p, t).wait_recv()
            total = total + dot_nt(others[p - 1, t], q_other[p - 1])
        return factor * total

    def note_top(value):
        top_ref[0:1, :] = jnp.maximum(top_ref[0:1, :], jnp.max(value, axis=0, keepdims=True))

    def score_negative(t):
        ok = neg[me, partner(t * mp + mine)] >= 0
        value = jnp.where(ok, score(t), F32(-1e30))
        scores[t] = value
        note_top(value)

    def is_target(t):
        row = lax.broadcasted_iota(jnp.int32, (PBS, rows), 0) + (t * mp + mine - dp) * PBS
        return row == lax.broadcasted_iota(jnp.int32, (PBS, rows), 1)

    own = jnp.zeros((1, rows), F32)
    for t in range(neg_groups, groups):
        value = score(t)
        scores[t] = value
        note_top(value)
        own = own + jnp.sum(jnp.where(is_target(t), value, F32(0.0)), axis=0, keepdims=True)
    stats[mine, 2:3, :] = own

    @pl.loop(0, neg_groups)
    def _(k):
        t = ordered(k)
        for c in range(mp):
            @pl.when(t * mp + c > 0)
            def _():
                fetch(t * mp + c).wait_recv()
        for p in range(1, mp):
            relay(p, t).start()

        @pl.when(k > 0)
        def _():
            score_negative(ordered(k - 1))

    score_negative(ordered(neg_groups - 1))

    top = top_ref[0:1, :]

    @pl.loop(0, groups, init_carry=jnp.zeros((1, rows), F32))
    def total(t, carry):
        return carry + jnp.sum(jnp.exp(scores[t] - top), axis=0, keepdims=True)

    stats[mine, 0:1, :] = top
    stats[mine, 1:2, :] = total
    for p in range(1, mp):
        share_stats(p).start()
    for p in range(1, mp):
        stats_from(p).wait_recv()
    whole_top = stats[0, 0:1, :]
    for i in range(1, mp):
        whole_top = jnp.maximum(whole_top, stats[i, 0:1, :])
    whole = jnp.zeros((1, rows), F32)
    own_score = jnp.zeros((1, rows), F32)
    for i in range(mp):
        whole = whole + stats[i, 1:2, :] * jnp.exp(stats[i, 0:1, :] - whole_top)
        own_score = own_score + stats[i, 2:3, :]
    lse = whole_top + jnp.log(whole)
    losses[...] = lse - own_score
    top_ref[1:2, :] = lse

    def candidate_grad(i):
        return factor * jnp.dot(grads[i], q[...], preferred_element_type=F32)

    def send_back(s):
        back[s] = candidate_grad(s).astype(BF16)

        @pl.when(s > 0)
        def _():
            give_back(s).start()

    @pl.loop(0, neg_groups)
    def _(k):
        t = ordered(k)
        grads[t * mp + mine] = jnp.exp(scores[t] - top_ref[1:2, :]).astype(BF16)
        for p in range(1, mp):
            share_grads(p, t).start()
        send_back(t * mp + mine)

    for t in range(neg_groups, groups):
        prob = jnp.exp(scores[t] - top_ref[1:2, :])
        grads[t * mp + mine] = (prob - jnp.where(is_target(t), F32(1.0), F32(0.0))).astype(BF16)
        for p in range(1, mp):
            share_grads(p, t).start()

    @pl.loop(0, neg_groups)
    def _(k):
        t = ordered(k)
        for p in range(1, mp):
            grads_from(p, t).wait_recv()
            send_back(t * mp + lax.rem(mine + mp - p, mp))

    keep = pltpu.make_async_copy(back.at[0], returned.at[0], load_sem)
    keep.start()
    for t in range(neg_groups, groups):
        for p in range(1, mp):
            grads_from(p, t).wait_recv()
    for b in range(pos_blocks):
        pos_grad[b * PBS:(b + 1) * PBS, :] = candidate_grad(dp + b)
    query_grad[...] = jnp.zeros_like(query_grad)

    @pl.loop(0, groups)
    def _(t):
        g = grads[pl.ds(t * mp, mp)].reshape(mp * PBS, rows)
        c = cands[pl.ds(t * mp, mp)].reshape(mp * PBS, width)
        query_grad[...] += factor * lax.dot_general(
            g, c, (((0,), (0,)), ((), ())), preferred_element_type=F32)

    keep.wait()

    @pl.loop(1, dp)
    def _(s):
        fetch(s).wait_send()
        give_back(s).wait()

    for p in range(1, mp):
        share_queries(p).wait_send()
        share_stats(p).wait_send()

        @pl.loop(0, groups)
        def _(t):
            relay(p, t).wait_send()
            share_grads(p, t).wait_send()


def assemble_kernel(dp, per, me_ref, neg, pos, pos_grad, returned, out, high, low):
    step = pl.program_id(0)
    me = me_ref[0]
    rows, width = pos_grad.shape
    span = per * PBS

    @pl.when(step == 0)
    def _():
        value = pos_grad[...]
        top = value.astype(BF16)
        high[...] = top
        low[...] = (value - top.astype(F32)).astype(BF16)

    ids = lax.broadcasted_iota(jnp.int32, (span, rows), 0) + step * span
    pick = jnp.where(ids == pos[...], 1.0, 0.0).astype(BF16)
    value = jnp.dot(pick, high[...], preferred_element_type=F32) + jnp.dot(
        pick, low[...], preferred_element_type=F32)
    out[...] = value.reshape(per, PBS, width)

    @pl.loop(0, dp)
    def _(s):
        block = neg[me ^ s, me] - step * per

        @pl.when((block >= 0) & (block < per))
        def _():
            out[block] += returned[s].astype(F32)


def body(queries, passages, positives, negatives):
    dp = lax.axis_size("dp")
    mp = lax.axis_size("mp")
    rows, width = queries.shape
    factor = (width * mp) ** (-0.5)
    block_count = passages.shape[0] // PBS
    blocks = passages.reshape(block_count, PBS, width)
    total_blocks = dp + rows // PBS
    groups = total_blocks // mp
    vmem = pl.BlockSpec(memory_space=pltpu.VMEM)
    smem = pl.BlockSpec(memory_space=pltpu.SMEM)
    anywhere = pl.BlockSpec(memory_space=pl.ANY)
    dma = pltpu.SemaphoreType.DMA
    losses, query_grad, pos_grad, returned = pl.pallas_call(
        functools.partial(exchange_kernel, dp, mp, factor),
        out_shape=(
            jax.ShapeDtypeStruct((1, rows), F32),
            jax.ShapeDtypeStruct((rows, width), F32),
            jax.ShapeDtypeStruct((rows, width), F32),
            jax.ShapeDtypeStruct((dp, PBS, width), BF16),
        ),
        in_specs=[smem, vmem, vmem, anywhere],
        out_specs=(vmem, vmem, vmem, anywhere),
        scratch_shapes=[
            pltpu.VMEM((block_count, PBS, width), BF16),
            pltpu.VMEM((dp, PBS, width), BF16),
            pltpu.VMEM((total_blocks, PBS, width), BF16),
            pltpu.VMEM((mp - 1, groups, PBS, width), BF16),
            pltpu.VMEM((mp - 1, rows, width), BF16),
            pltpu.VMEM((groups, PBS, rows), F32),
            pltpu.VMEM((total_blocks, PBS, rows), BF16),
            pltpu.VMEM((dp, PBS, width), BF16),
            pltpu.VMEM((mp, 8, rows), F32),
            pltpu.VMEM((8, rows), F32),
            dma, dma((dp,)), dma((dp,)), dma((mp - 1, groups)), dma((mp - 1, groups)),
            dma((mp - 1,)), dma((mp - 1,)), dma((mp - 1,)), dma((mp - 1,)),
            dma((mp - 1, groups)), dma((mp - 1, groups)), dma((dp,)), dma((dp,)),
        ],
        compiler_params=pltpu.CompilerParams(
            collective_id=0, has_side_effects=True, vmem_limit_bytes=50 * 2**20),
    )(negatives, positives.reshape(rows, 1), queries, blocks)
    per = 4
    whole = lambda *shape: pl.BlockSpec(shape, lambda k: (0,) * len(shape))
    passage_grad = pl.pallas_call(
        functools.partial(assemble_kernel, dp, per),
        grid=(block_count // per,),
        out_shape=jax.ShapeDtypeStruct((block_count, PBS, width), F32),
        in_specs=[smem, smem, whole(1, rows), whole(rows, width), whole(dp, PBS, width)],
        out_specs=pl.BlockSpec((per, PBS, width), lambda k: (k, 0, 0)),
        scratch_shapes=[pltpu.VMEM((rows, width), BF16), pltpu.VMEM((rows, width), BF16)],
        compiler_params=pltpu.CompilerParams(vmem_limit_bytes=40 * 2**20),
    )(lax.axis_index("dp").reshape(1).astype(jnp.int32), negatives,
      positives.reshape(1, rows), pos_grad, returned)
    return losses.reshape(rows), query_grad, passage_grad.reshape(block_count * PBS, width)


def solution(mesh):
    in_specs = (P("dp", "mp"), P("dp", "mp"), P("dp"), P())
    out_specs = (P("dp"), P("dp", "mp"), P("dp", "mp"))
    return jax.shard_map(body, mesh=mesh, in_specs=in_specs, out_specs=out_specs, check_vma=False)
```

time: 281 us -> 128 us (0.46)
  waiting for transfers between devices: 186 us -> 0 us
  Pallas kernels: 0 us -> 121 us
  other arithmetic: 22.6 us -> 0 us
  matrix products: 15.1 us -> 0 us
  local copies, waits for them, and re-layouts: 19.8 us -> 5.75 us
  between operations: 14.2 us -> 0.68 us
  starting transfers between devices: 13.3 us -> 0 us
  blocking collectives: 9.95 us -> 0 us
    pallas_call x0 -> x2, Pallas kernels: none -> 121 us  [the longest x1 111 us: body(): pl.pallas_call(functools.partial(exchange_kernel, dp, mp, factor), out_sh...]
    all_to_all x2 -> x0, waiting for transfers between devices: 80 us -> none  [the longest x1 41.7 us: body(): lax.all_to_all(outgoing, 'dp', split_axis=0, concat_axis=0, tiled=True)]
    reduce_scatter x1 -> x0, waiting for transfers between devices: 64.4 us -> none  [body(): lax.psum_scatter(lax.dot_general(cands, queries, (((1,), (1,)), ((), ()))...]
    all_gather x1 -> x0, waiting for transfers between devices: 41.5 us -> none  [body(): all_grads = lax.all_gather(grad_scores, 'mp', axis=0, tiled=True)]
    dot_general x4 -> x0, matrix products: 15.1 us -> none  [the longest x1 5.31 us: body(): lax.dot_general(cands, queries, (((1,), (1,)), ((), ())), preferred_eleme...]
    all_to_all x2 -> x0, starting transfers between devices: 13.2 us -> none  [the longest x1 6.69 us: body(): lax.all_to_all(outgoing, 'dp', split_axis=0, concat_axis=0, tiled=True)]
    scatter-add x1 -> x0, other arithmetic: 11 us -> none  [body(): block_grad.reshape(block_count * PBS, shard_width).at[positives]]
    all_gather x3 -> x0, blocking collectives: 9.95 us -> none  [combined_all(): gathered = jax.tree.map(lambda a: lax.all_gather(a, axis), part)]
  transfers between devices with their start and end apart: 4 -> 0, of which waited for: 4 -> 0; matrix products, arithmetic and copies ran while one was open for 4% -> 0% of each run, Pallas kernels for 0% -> 0%
where the time goes in v1:
time: 128 us
  Pallas kernels  121 us (95%)
  local copies, waits for them, and re-layouts  5.75 us (4%)
    pallas_call x1, Pallas kernels, body(): pl.pallas_call(functools.partial(exchange_kernel, dp, mp, factor), out_sh...  111 us
    pallas_call x1, Pallas kernels, body(): pl.pallas_call(functools.partial(assemble_kernel, dp, per), grid=(block_c...  10 us
    unnamed x10, local copies, waits for them, and re-layouts  4.87 us

profile of v1, /device:TPU:13, one launch (start us, length us, event | category | flops | bytes accessed | tf_op | source)
XLA Modules:
  0.0 127.7 jit_solution(11973943314701340829)
XLA Ops:
  0.6 0.0 copy-start.3
  0.6 0.9 copy.7.pos
  1.5 0.0 copy-start.1
  1.5 1.0 copy-done.1
  2.6 0.0 copy-start.2
  2.6 0.7 copy-done.2
  3.3 111.2 %shard_map.67 = (f32[1,512]{1,0:T(1,128)S(1)}, f32[512,512]{1,0:T(8,128)S(1)}, f32[512,512]{1,0:T(8,128)S(1)}, bf16[16,128,512]{2,1,0:T(8,128)(2,1)}) custom-call(s32[16,16]{1,0:T(8,128)S(1)} %copy-done.2, s32[512,1]{1,0:T(8,128)S(1)} %copy.7.pos, bf16[512,512]{1,0:T(8,128)(2,1)S(1)} %copy-done.1, bf16[32,128,512]{2,1,0:T(8,128)(2,1)} %bitcast.10), custom_call_target="tpu_custom_call" | custom-call | tf_op jit(solution)/shard_map/pallas_call | solution.py:324
  114.5 0.0 copy-done.3
  114.5 0.0 copy-start
  114.5 1.6 %copy-done = bf16[16,128,512]{2,1,0:T(8,128)(2,1)S(1)} copy-done((bf16[16,128,512]{2,1,0:T(8,128)(2,1)S(1)}, bf16[16,128,512]{2,1,0:T(8,128)(2,1)}, u32[]{:S(2)}) %copy-start) | copy-done | bytes 2097176
  116.1 10.0 %shard_map.68 = f32[32,128,512]{2,1,0:T(8,128)} custom-call(s32[1]{0:T(128)} %bitcast.3.me_ref, s32[16,16]{1,0:T(8,128)S(1)} %copy-done.2, s32[1,512]{1,0:T(1,128)S(1)} %bitcast.7, f32[512,512]{1,0:T(8,128)S(1)} %get-tuple-element.9.pos_grad, bf16[16,128,512]{2,1,0:T(8,128)(2,1)S(1)} %copy-done), custom_call_target="tpu_custom_call" | custom-call | tf_op jit(solution)/shard_map/pallas_call | solution.py:354
  126.1 0.6 copy.10
  126.7 1.0 copy.11
Async XLA Ops:
  0.6 113.9 %copy-start.3 = (s32[512]{0:T(512)S(1)}, s32[512]{0:T(512)}, u32[]{:S(2)}) copy-start(s32[512]{0:T(512)} %param.6) | copy-start | bytes 6148
  1.5 1.0 copy-start.1
  2.6 0.7 copy-start.2
  114.5 1.6 %copy-start = (bf16[16,128,512]{2,1,0:T(8,128)(2,1)S(1)}, bf16[16,128,512]{2,1,0:T(8,128)(2,1)}, u32[]{:S(2)}) copy-start(bf16[16,128,512]{2,1,0:T(8,128)(2,1)} %get-tuple-element.10.returned) | copy-start | bytes 6291460

commit v2 on v1

--- a/solution.py
+++ b/solution.py
@@ -1,4 +1,5 @@
 import functools
+import math
 
 import jax
 import jax.numpy as jnp
@@ -15,10 +16,10 @@
 
 def exchange_kernel(
     dp, mp, factor,
-    neg, pos, q, passages,
-    losses, query_grad, pos_grad, returned,
-    table, sending, cands, others, q_other, scores, grads, back, stats, top_ref,
-    load_sem, f_send, f_recv, x_send, x_recv, q_send, q_recv,
+    neg_hbm, pos_hbm, q_hbm, passages,
+    losses, query_grad, base, returned,
+    neg, pos, q, high, low, table, sending, cands, others, q_other, scores, grads, back, stats, top_ref,
+    load_sem, neg_sem, pos_sem, q_sem, f_send, f_recv, x_send, x_recv, q_send, q_recv,
     s_send, s_recv, g_send, g_recv, r_send, r_recv,
 ):
     me = lax.axis_index("dp")
@@ -95,6 +96,12 @@
 
     load = pltpu.make_async_copy(passages, table, load_sem)
     load.start()
+    load_neg = pltpu.make_async_copy(neg_hbm, neg, neg_sem)
+    load_neg.start()
+    load_q = pltpu.make_async_copy(q_hbm, q, q_sem)
+    load_q.start()
+    load_pos = pltpu.make_async_copy(pos_hbm, pos, pos_sem)
+    load_pos.start()
     barrier = pltpu.get_barrier_semaphore()
 
     @pl.loop(1, dp)
@@ -103,6 +110,9 @@
 
     for p in range(1, mp):
         pl.semaphore_signal(barrier, inc=1, device_id=(me, peer(p)), device_id_type=MESH)
+    load_neg.wait()
+    load_q.wait()
+    load_pos.wait()
     load.wait()
     pl.semaphore_wait(barrier, dp - 1 + mp - 1)
 
@@ -128,10 +138,13 @@
     query_grad[...] = jnp.zeros_like(query_grad)
     chunk = 4 * PBS
 
+    column = jnp.transpose(jnp.broadcast_to(pos[...].astype(F32), (PBS, rows)))[:, 0:1]
+    column = column.astype(jnp.int32)
+
     @pl.loop(0, table.shape[0] // 4)
     def _(c):
         ids = lax.broadcasted_iota(jnp.int32, (rows, chunk), 1) + c * chunk
-        pick = jnp.where(ids == pos[...], 1.0, 0.0).astype(BF16)
+        pick = jnp.where(ids == column, 1.0, 0.0).astype(BF16)
         part = table[pl.ds(c * 4, 4)].reshape(chunk, width)
         query_grad[...] += jnp.dot(pick, part, preferred_element_type=F32)
 
@@ -220,11 +233,16 @@
         return factor * jnp.dot(grads[i], q[...], preferred_element_type=F32)
 
     def send_back(s):
-        back[s] = candidate_grad(s).astype(BF16)
+        value = candidate_grad(s).astype(BF16)
 
         @pl.when(s > 0)
         def _():
+            back[s] = value
             give_back(s).start()
+
+        @pl.when(s == 0)
+        def _():
+            returned[0] = value
 
     @pl.loop(0, neg_groups)
     def _(k):
@@ -247,13 +265,23 @@
             grads_from(p, t).wait_recv()
             send_back(t * mp + lax.rem(mine + mp - p, mp))
 
-    keep = pltpu.make_async_copy(back.at[0], returned.at[0], load_sem)
-    keep.start()
     for t in range(neg_groups, groups):
         for p in range(1, mp):
             grads_from(p, t).wait_recv()
     for b in range(pos_blocks):
-        pos_grad[b * PBS:(b + 1) * PBS, :] = candidate_grad(dp + b)
+        value = candidate_grad(dp + b)
+        upper = value.astype(BF16)
+        high[b * PBS:(b + 1) * PBS, :] = upper
+        low[b * PBS:(b + 1) * PBS, :] = (value - upper.astype(F32)).astype(BF16)
+
+    @pl.loop(0, table.shape[0] // 4)
+    def _(c):
+        ids = lax.broadcasted_iota(jnp.int32, (chunk, rows), 0) + c * chunk
+        pick = jnp.where(ids == pos[...], 1.0, 0.0).astype(BF16)
+        value = jnp.dot(pick, high[...], preferred_element_type=F32) + jnp.dot(
+            pick, low[...], preferred_element_type=F32)
+        base[pl.ds(c * 4, 4)] = value.reshape(4, PBS, width)
+
     query_grad[...] = jnp.zeros_like(query_grad)
 
     @pl.loop(0, groups)
@@ -263,8 +291,6 @@
         query_grad[...] += factor * lax.dot_general(
             g, c, (((0,), (0,)), ((), ())), preferred_element_type=F32)
 
-    keep.wait()
-
     @pl.loop(1, dp)
     def _(s):
         fetch(s).wait_send()
@@ -280,32 +306,71 @@
             share_grads(p, t).wait_send()
 
 
-def assemble_kernel(dp, per, me_ref, neg, pos, pos_grad, returned, out, high, low):
-    step = pl.program_id(0)
+def assemble_kernel(
+    dp, me_ref, neg, losses_in, query_grad_in, base, returned,
+    losses, query_grad, out, stage, state, sems, loss_sem, query_sem,
+):
     me = me_ref[0]
-    rows, width = pos_grad.shape
-    span = per * PBS
-
-    @pl.when(step == 0)
-    def _():
-        value = pos_grad[...]
-        top = value.astype(BF16)
-        high[...] = top
-        low[...] = (value - top.astype(F32)).astype(BF16)
-
-    ids = lax.broadcasted_iota(jnp.int32, (span, rows), 0) + step * span
-    pick = jnp.where(ids == pos[...], 1.0, 0.0).astype(BF16)
-    value = jnp.dot(pick, high[...], preferred_element_type=F32) + jnp.dot(
-        pick, low[...], preferred_element_type=F32)
-    out[...] = value.reshape(per, PBS, width)
+    block_count = base.shape[0]
+    keep_losses = pltpu.make_async_copy(losses_in, losses, loss_sem)
+    keep_losses.start()
+    keep_query = pltpu.make_async_copy(query_grad_in, query_grad, query_sem)
+    keep_query.start()
+
+    @pl.loop(0, block_count)
+    def _(k):
+        state[k] = 0
 
     @pl.loop(0, dp)
     def _(s):
-        block = neg[me ^ s, me] - step * per
-
-        @pl.when((block >= 0) & (block < per))
-        def _():
-            out[block] += returned[s].astype(F32)
+        k = neg[me ^ s, me]
+
+        @pl.when(k >= 0)
+        def _():
+            state[k] = 1
+
+    def plain(k):
+        return pltpu.make_async_copy(base.at[k], out.at[k], sems.at[k])
+
+    @pl.loop(0, block_count)
+    def _(k):
+        @pl.when(state[k] == 0)
+        def _():
+            plain(k).start()
+
+    @pl.loop(0, dp)
+    def _(s):
+        k = neg[me ^ s, me]
+
+        @pl.when(k >= 0)
+        def _():
+            now = state[k]
+
+            @pl.when(now == 1)
+            def _():
+                state[k] = 2 + s
+                stage[s] = base[k] + returned[s].astype(F32)
+
+            @pl.when(now > 1)
+            def _():
+                stage[now - 2] += returned[s].astype(F32)
+
+    @pl.loop(0, dp)
+    def _(s):
+        k = neg[me ^ s, me]
+
+        @pl.when(k >= 0)
+        def _():
+            @pl.when(state[k] == 2 + s)
+            def _():
+                pltpu.make_async_copy(stage.at[s], out.at[k], sems.at[k]).start()
+
+    keep_losses.wait()
+    keep_query.wait()
+
+    @pl.loop(0, block_count)
+    def _(k):
+        plain(k).wait()
 
 
 def body(queries, passages, positives, negatives):
@@ -319,48 +384,60 @@
     groups = total_blocks // mp
     vmem = pl.BlockSpec(memory_space=pltpu.VMEM)
     smem = pl.BlockSpec(memory_space=pltpu.SMEM)
-    anywhere = pl.BlockSpec(memory_space=pl.ANY)
+    hbm = pl.BlockSpec(memory_space=pltpu.HBM)
     dma = pltpu.SemaphoreType.DMA
-    losses, query_grad, pos_grad, returned = pl.pallas_call(
+    made = (
+        jax.ShapeDtypeStruct((1, rows), F32),
+        jax.ShapeDtypeStruct((rows, width), F32),
+        jax.ShapeDtypeStruct((block_count, PBS, width), F32),
+        jax.ShapeDtypeStruct((dp, PBS, width), BF16),
+    )
+    scratch = [
+        pltpu.VMEM((1, rows), jnp.int32),
+        pltpu.VMEM((rows, width), BF16),
+        pltpu.VMEM((rows, width), BF16),
+        pltpu.VMEM((rows, width), BF16),
+        pltpu.VMEM((block_count, PBS, width), BF16),
+        pltpu.VMEM((dp, PBS, width), BF16),
+        pltpu.VMEM((total_blocks, PBS, width), BF16),
+        pltpu.VMEM((mp - 1, groups, PBS, width), BF16),
+        pltpu.VMEM((mp - 1, rows, width), BF16),
+        pltpu.VMEM((groups, PBS, rows), F32),
+        pltpu.VMEM((total_blocks, PBS, rows), BF16),
+        pltpu.VMEM((dp, PBS, width), BF16),
+        pltpu.VMEM((mp, 8, rows), F32),
+        pltpu.VMEM((8, rows), F32),
+    ]
+    held = sum(math.prod(a.shape) * jnp.dtype(a.dtype).itemsize for a in (*made, *scratch))
+    losses, query_grad, base, returned = pl.pallas_call(
         functools.partial(exchange_kernel, dp, mp, factor),
-        out_shape=(
-            jax.ShapeDtypeStruct((1, rows), F32),
-            jax.ShapeDtypeStruct((rows, width), F32),
-            jax.ShapeDtypeStruct((rows, width), F32),
-            jax.ShapeDtypeStruct((dp, PBS, width), BF16),
-        ),
-        in_specs=[smem, vmem, vmem, anywhere],
-        out_specs=(vmem, vmem, vmem, anywhere),
+        out_shape=made,
+        in_specs=[hbm, hbm, hbm, hbm],
+        out_specs=(vmem, vmem, vmem, vmem),
         scratch_shapes=[
-            pltpu.VMEM((block_count, PBS, width), BF16),
-            pltpu.VMEM((dp, PBS, width), BF16),
-            pltpu.VMEM((total_blocks, PBS, width), BF16),
-            pltpu.VMEM((mp - 1, groups, PBS, width), BF16),
-            pltpu.VMEM((mp - 1, rows, width), BF16),
-            pltpu.VMEM((groups, PBS, rows), F32),
-            pltpu.VMEM((total_blocks, PBS, rows), BF16),
-            pltpu.VMEM((dp, PBS, width), BF16),
-            pltpu.VMEM((mp, 8, rows), F32),
-            pltpu.VMEM((8, rows), F32),
-            dma, dma((dp,)), dma((dp,)), dma((mp - 1, groups)), dma((mp - 1, groups)),
+            pltpu.SMEM((dp, dp), jnp.int32),
+            *scratch,
+            dma, dma, dma, dma,
+            dma((dp,)), dma((dp,)), dma((mp - 1, groups)), dma((mp - 1, groups)),
             dma((mp - 1,)), dma((mp - 1,)), dma((mp - 1,)), dma((mp - 1,)),
             dma((mp - 1, groups)), dma((mp - 1, groups)), dma((dp,)), dma((dp,)),
         ],
         compiler_params=pltpu.CompilerParams(
-            collective_id=0, has_side_effects=True, vmem_limit_bytes=50 * 2**20),
-    )(negatives, positives.reshape(rows, 1), queries, blocks)
-    per = 4
-    whole = lambda *shape: pl.BlockSpec(shape, lambda k: (0,) * len(shape))
-    passage_grad = pl.pallas_call(
-        functools.partial(assemble_kernel, dp, per),
-        grid=(block_count // per,),
-        out_shape=jax.ShapeDtypeStruct((block_count, PBS, width), F32),
-        in_specs=[smem, smem, whole(1, rows), whole(rows, width), whole(dp, PBS, width)],
-        out_specs=pl.BlockSpec((per, PBS, width), lambda k: (k, 0, 0)),
-        scratch_shapes=[pltpu.VMEM((rows, width), BF16), pltpu.VMEM((rows, width), BF16)],
-        compiler_params=pltpu.CompilerParams(vmem_limit_bytes=40 * 2**20),
+            collective_id=0, has_side_effects=True, vmem_limit_bytes=held + 4 * 2**20),
+    )(*(pltpu.with_memory_space_constraint(a, pltpu.HBM) for a in (negatives, positives.reshape(1, rows), queries, blocks)))
+    losses, query_grad, passage_grad = pl.pallas_call(
+        functools.partial(assemble_kernel, dp),
+        out_shape=made[:3],
+        in_specs=[smem, smem, vmem, vmem, vmem, vmem],
+        out_specs=(hbm, hbm, hbm),
+        scratch_shapes=[
+            pltpu.VMEM((dp, PBS, width), F32),
+            pltpu.SMEM((block_count,), jnp.int32),
+            dma((block_count,)), dma, dma,
+        ],
+        compiler_params=pltpu.CompilerParams(vmem_limit_bytes=24 * 2**20),
     )(lax.axis_index("dp").reshape(1).astype(jnp.int32), negatives,
-      positives.reshape(1, rows), pos_grad, returned)
+      losses, query_grad, base, returned)
     return losses.reshape(rows), query_grad, passage_grad.reshape(block_count * PBS, width)
 
 

time: 128 us -> 117 us (0.914)
  Pallas kernels: 121 us -> 115 us
  local copies, waits for them, and re-layouts: 5.75 us -> 0.69 us
    pallas_call x1, Pallas kernels: 10 us -> 4.63 us  [body(): pl.pallas_call(functools.partial(assemble_kernel, dp), out_shape=made[:3]...]
    unnamed x10 -> x2, local copies, waits for them, and re-layouts: 4.87 us -> 0.69 us
where the time goes in v2:
time: 117 us; the launch traced here: 116 us
  Pallas kernels  115 us (98%)
    pallas_call x1, Pallas kernels, body(): pl.pallas_call(functools.partial(exchange_kernel, dp, mp, factor), out_sh...  111 us
    pallas_call x1, Pallas kernels, body(): pl.pallas_call(functools.partial(assemble_kernel, dp), out_shape=made[:3]...  4.63 us

profile of v2, /device:TPU:13, one launch (start us, length us, event | category | flops | bytes accessed | tf_op | source)
XLA Modules:
  0.0 116.5 jit_solution(8502403389164622578)
XLA Ops:
  0.6 110.5 %shard_map.67 = (f32[1,512]{1,0:T(1,128)S(1)}, f32[512,512]{1,0:T(8,128)S(1)}, f32[32,128,512]{2,1,0:T(8,128)S(1)}, bf16[16,128,512]{2,1,0:T(8,128)(2,1)S(1)}) custom-call(s32[16,16]{1,0:T(8,128)} %neg.1, s32[1,512]{1,0:T(1,128)} %bitcast.6, bf16[512,512]{1,0:T(8,128)(2,1)} %q_hbm.1, bf16[32,128,512]{2,1,0:T(8,128)(2,1)} %bitcast.5), custom_call_target="tpu_custom_call" | custom-call | tf_op jit(solution)/shard_map/pallas_call | solution.py:412
  111.2 0.0 copy-start
  111.2 0.7 copy-done
  111.9 4.6 %shard_map.68 = (f32[1,512]{1,0:T(1,128)}, f32[512,512]{1,0:T(8,128)}, f32[32,128,512]{2,1,0:T(8,128)}) custom-call(s32[1]{0:T(128)} %bitcast.me_ref, s32[16,16]{1,0:T(8,128)S(1)} %copy-done, f32[1,512]{1,0:T(1,128)S(1)} %get-tuple-element.10.losses_in, f32[512,512]{1,0:T(8,128)S(1)} %get-tuple-element.11.query_grad_in, ...), custom_call_target="tpu_custom_call" | custom-call | tf_op jit(solution)/shard_map/pallas_call | solution.py:428
Async XLA Ops:
  111.2 0.7 copy-start

commit v3 on v2

--- a/solution.py
+++ b/solution.py
@@ -9,6 +9,9 @@
 from jax.sharding import PartitionSpec as P
 
 PBS = 128
+WINDOW = 4
+LAG = 2
+FIRST = 2
 MESH = pl.DeviceIdType.MESH
 F32 = jnp.float32
 BF16 = jnp.bfloat16
@@ -121,16 +124,20 @@
 
     cands[0] = block_for(0)
 
-    @pl.loop(0, neg_groups)
-    def _(k):
-        t = ordered(k)
+    window = min(WINDOW, neg_groups)
+
+    def send_group(k):
         for c in range(mp):
-            s = t * mp + c
+            s = ordered(k) * mp + c
 
             @pl.when(s > 0)
             def _():
                 sending[s] = block_for(s)
                 fetch(s).start()
+
+    @pl.loop(0, window)
+    def _(k):
+        send_group(k)
 
     for p in range(1, mp):
         share_queries(p).start()
@@ -157,6 +164,7 @@
         share_queries(p).wait_recv()
 
     top_ref[...] = jnp.full(top_ref.shape, -1e30, F32)
+    top_ref[2:3, :] = jnp.zeros((1, rows), F32)
 
     def dot_nt(a, b):
         return lax.dot_general(a, b, (((1,), (1,)), ((), ())), preferred_element_type=F32)
@@ -168,29 +176,25 @@
             total = total + dot_nt(others[p - 1, t], q_other[p - 1])
         return factor * total
 
-    def note_top(value):
-        top_ref[0:1, :] = jnp.maximum(top_ref[0:1, :], jnp.max(value, axis=0, keepdims=True))
-
-    def score_negative(t):
+    def note(value):
+        before = top_ref[0:1, :]
+        now = jnp.maximum(before, jnp.max(value, axis=0, keepdims=True))
+        part = jnp.sum(jnp.exp(value - now), axis=0, keepdims=True)
+        top_ref[2:3, :] = top_ref[2:3, :] * jnp.exp(before - now) + part
+        top_ref[0:1, :] = now
+
+    def score_negative(k):
+        t = ordered(k)
         ok = neg[me, partner(t * mp + mine)] >= 0
         value = jnp.where(ok, score(t), F32(-1e30))
         scores[t] = value
-        note_top(value)
+        note(value)
 
     def is_target(t):
         row = lax.broadcasted_iota(jnp.int32, (PBS, rows), 0) + (t * mp + mine - dp) * PBS
         return row == lax.broadcasted_iota(jnp.int32, (PBS, rows), 1)
 
-    own = jnp.zeros((1, rows), F32)
-    for t in range(neg_groups, groups):
-        value = score(t)
-        scores[t] = value
-        note_top(value)
-        own = own + jnp.sum(jnp.where(is_target(t), value, F32(0.0)), axis=0, keepdims=True)
-    stats[mine, 2:3, :] = own
-
-    @pl.loop(0, neg_groups)
-    def _(k):
+    def arrive(k):
         t = ordered(k)
         for c in range(mp):
             @pl.when(t * mp + c > 0)
@@ -199,20 +203,37 @@
         for p in range(1, mp):
             relay(p, t).start()
 
-        @pl.when(k > 0)
-        def _():
-            score_negative(ordered(k - 1))
-
-    score_negative(ordered(neg_groups - 1))
-
-    top = top_ref[0:1, :]
-
-    @pl.loop(0, groups, init_carry=jnp.zeros((1, rows), F32))
-    def total(t, carry):
-        return carry + jnp.sum(jnp.exp(scores[t] - top), axis=0, keepdims=True)
-
-    stats[mine, 0:1, :] = top
-    stats[mine, 1:2, :] = total
+        @pl.when(k + window < neg_groups)
+        def _():
+            send_group(k + window)
+
+    @pl.loop(0, half)
+    def _(k):
+        arrive(k)
+
+    own = jnp.zeros((1, rows), F32)
+    for t in range(neg_groups, groups):
+        value = score(t)
+        scores[t] = value
+        note(value)
+        own = own + jnp.sum(jnp.where(is_target(t), value, F32(0.0)), axis=0, keepdims=True)
+    stats[mine, 2:3, :] = own
+
+    @pl.loop(0, half - LAG)
+    def _(k):
+        score_negative(k)
+
+    @pl.loop(half, neg_groups)
+    def _(k):
+        arrive(k)
+        score_negative(k - LAG)
+
+    @pl.loop(neg_groups - LAG, neg_groups)
+    def _(k):
+        score_negative(k)
+
+    stats[mine, 0:1, :] = top_ref[0:1, :]
+    stats[mine, 1:2, :] = top_ref[2:3, :]
     for p in range(1, mp):
         share_stats(p).start()
     for p in range(1, mp):
@@ -244,13 +265,29 @@
         def _():
             returned[0] = value
 
-    @pl.loop(0, neg_groups)
-    def _(k):
+    def share_negative(k):
         t = ordered(k)
         grads[t * mp + mine] = jnp.exp(scores[t] - top_ref[1:2, :]).astype(BF16)
         for p in range(1, mp):
             share_grads(p, t).start()
         send_back(t * mp + mine)
+
+    def add_query_grad(t):
+        g = grads[pl.ds(t * mp, mp)].reshape(mp * PBS, rows)
+        c = cands[pl.ds(t * mp, mp)].reshape(mp * PBS, width)
+        query_grad[...] += factor * lax.dot_general(
+            g, c, (((0,), (0,)), ((), ())), preferred_element_type=F32)
+
+    def finish_negative(k):
+        t = ordered(k)
+        for p in range(1, mp):
+            grads_from(p, t).wait_recv()
+            send_back(t * mp + lax.rem(mine + mp - p, mp))
+        add_query_grad(t)
+
+    @pl.loop(0, FIRST)
+    def _(k):
+        share_negative(k)
 
     for t in range(neg_groups, groups):
         prob = jnp.exp(scores[t] - top_ref[1:2, :])
@@ -258,12 +295,15 @@
         for p in range(1, mp):
             share_grads(p, t).start()
 
-    @pl.loop(0, neg_groups)
-    def _(k):
-        t = ordered(k)
-        for p in range(1, mp):
-            grads_from(p, t).wait_recv()
-            send_back(t * mp + lax.rem(mine + mp - p, mp))
+    @pl.loop(FIRST, neg_groups)
+    def _(k):
+        share_negative(k)
+
+    query_grad[...] = jnp.zeros_like(query_grad)
+
+    @pl.loop(0, FIRST)
+    def _(k):
+        finish_negative(k)
 
     for t in range(neg_groups, groups):
         for p in range(1, mp):
@@ -273,6 +313,14 @@
         upper = value.astype(BF16)
         high[b * PBS:(b + 1) * PBS, :] = upper
         low[b * PBS:(b + 1) * PBS, :] = (value - upper.astype(F32)).astype(BF16)
+
+    @pl.loop(FIRST, neg_groups)
+    def _(k):
+        finish_negative(k)
+
+    @pl.loop(neg_groups, groups)
+    def _(t):
+        add_query_grad(t)
 
     @pl.loop(0, table.shape[0] // 4)
     def _(c):
@@ -281,15 +329,6 @@
         value = jnp.dot(pick, high[...], preferred_element_type=F32) + jnp.dot(
             pick, low[...], preferred_element_type=F32)
         base[pl.ds(c * 4, 4)] = value.reshape(4, PBS, width)
-
-    query_grad[...] = jnp.zeros_like(query_grad)
-
-    @pl.loop(0, groups)
-    def _(t):
-        g = grads[pl.ds(t * mp, mp)].reshape(mp * PBS, rows)
-        c = cands[pl.ds(t * mp, mp)].reshape(mp * PBS, width)
-        query_grad[...] += factor * lax.dot_general(
-            g, c, (((0,), (0,)), ((), ())), preferred_element_type=F32)
 
     @pl.loop(1, dp)
     def _(s):

time: 117 us -> 115 us (0.983)
  Pallas kernels: 115 us -> 112 us
    pallas_call x1, Pallas kernels: 111 us -> 108 us  [body(): pl.pallas_call(functools.partial(exchange_kernel, dp, mp, factor), out_sh...]
where the time goes in v3:
time: 115 us; the launch traced here: 114 us
  Pallas kernels  112 us (97%)
    pallas_call x1, Pallas kernels, body(): pl.pallas_call(functools.partial(exchange_kernel, dp, mp, factor), out_sh...  108 us
    pallas_call x1, Pallas kernels, body(): pl.pallas_call(functools.partial(assemble_kernel, dp), out_shape=made[:3]...  4.6 us

profile of v3, /device:TPU:13, one launch (start us, length us, event | category | flops | bytes accessed | tf_op | source)
XLA Modules:
  0.0 113.8 jit_solution(9972482224560467558)
XLA Ops:
  0.6 107.9 %shard_map.67 = (f32[1,512]{1,0:T(1,128)S(1)}, f32[512,512]{1,0:T(8,128)S(1)}, f32[32,128,512]{2,1,0:T(8,128)S(1)}, bf16[16,128,512]{2,1,0:T(8,128)(2,1)S(1)}) custom-call(s32[16,16]{1,0:T(8,128)} %neg.1, s32[1,512]{1,0:T(1,128)} %bitcast.6, bf16[512,512]{1,0:T(8,128)(2,1)} %q_hbm.1, bf16[32,128,512]{2,1,0:T(8,128)(2,1)} %bitcast.5), custom_call_target="tpu_custom_call" | custom-call | tf_op jit(solution)/shard_map/pallas_call | solution.py:451
  108.5 0.0 copy-start
  108.5 0.7 copy-done
  109.2 4.6 %shard_map.68 = (f32[1,512]{1,0:T(1,128)}, f32[512,512]{1,0:T(8,128)}, f32[32,128,512]{2,1,0:T(8,128)}) custom-call(s32[1]{0:T(128)} %bitcast.me_ref, s32[16,16]{1,0:T(8,128)S(1)} %copy-done, f32[1,512]{1,0:T(1,128)S(1)} %get-tuple-element.10.losses_in, f32[512,512]{1,0:T(8,128)S(1)} %get-tuple-element.11.query_grad_in, ...), custom_call_target="tpu_custom_call" | custom-call | tf_op jit(solution)/shard_map/pallas_call | solution.py:467
Async XLA Ops:
  108.5 0.7 copy-start
